TPU v7x, 32 devices: a whole 2x2x4 slice. The times are simulated.
32 devices in a mesh: ty: 4 (over y, core), tx: 8 (over z, x).
Axes of the slice: x: 2, y: 2, z: 4, core: 2. Of those that a mesh axis runs over, the one named last changes fastest.
Arguments:
- object_re: float32 [2048, 4096], P('ty', 'tx'), may hold values from 0.5 to 1.5
- object_im: float32 [2048, 4096], P('ty', 'tx'), may hold values from -3 to 3
- probe_re: float32 [8, 128, 128], replicated, may hold values from -2 to 2
- probe_im: float32 [8, 128, 128], replicated, may hold values from -2 to 2
- patterns: float32 [4, 8, 16, 128, 128], P('ty', 'tx'), may hold values from 0.05 to 8
- offsets: int32 [4, 8, 16, 2], P('ty', 'tx'), may hold values from 0 to 511, as said below
- counts: int32 [4, 8, 8], P('ty', 'tx'), may hold values from 0 to 2, as said below
Outputs:
- new_object_re: float32 [2048, 4096], P('ty', 'tx')
- new_object_im: float32 [2048, 4096], P('ty', 'tx')
- new_probe_re: float32 [8, 128, 128], replicated
- new_probe_im: float32 [8, 128, 128], replicated
Inputs may be any that keep to these rules, and one draw needn't show every extreme that they name: Row offsets are below 512, column offsets below 512. `counts`: in every draw some reader receives 2 live scans from every owner tile of its row.
All inputs are finite; a program needn't handle non-finite values.
Results may differ from a plain program's by a relative error of at most 0.0001.
Values sent between devices are 32-bit elements; how exact they have to be, the bound alone decides.
A program may use at most 128 MiB of HBM per device.

v0:
```python
import math

import jax
import jax.numpy as jnp
import ml_dtypes
import numpy as np
from jax import lax
from jax.experimental import pallas as pl
from jax.experimental.pallas import tpu as pltpu
from jax.sharding import PartitionSpec as P

BF16 = jnp.bfloat16
F32 = jnp.float32
LANES = 128


def dft_tables(extent):
    k = np.arange(extent)
    angle = (k[:, None] * k[None, :] % extent) * (-2.0 * math.pi / extent)
    cos, sin = np.cos(angle) / math.sqrt(extent), np.sin(angle) / math.sqrt(extent)
    table = np.block([[cos, sin], [-sin, cos]])

    def parts(values):
        high = values.astype(np.float32).astype(ml_dtypes.bfloat16)
        low = (values - high.astype(np.float64)).astype(np.float32).astype(ml_dtypes.bfloat16)
        return high, low

    high, low = parts(table)
    flip_high, flip_low = parts(table.T)
    return (
        np.concatenate([high, high, low], axis=0),
        np.concatenate([flip_high, flip_high, flip_low], axis=1),
        np.concatenate([high, high, low], axis=1),
        np.concatenate([flip_high, flip_high, flip_low], axis=0),
    )


def split(value):
    high = value.astype(BF16)
    low = (value - high.astype(F32)).astype(BF16)
    return high, low


def right_product(real, imag, table):
    rh, rl = split(real)
    ih, il = split(imag)
    lhs = jnp.concatenate([rh, ih, rl, il, rh, ih], axis=1)
    return jnp.dot(lhs, table, preferred_element_type=F32)


def left_product(table, real, imag):
    rh, rl = split(real)
    ih, il = split(imag)
    rhs = jnp.concatenate([rh, ih, rl, il, rh, ih], axis=0)
    return jnp.dot(table, rhs, preferred_element_type=F32)


def main_kernel(
    offsets, counts, wide_re, wide_im, probe_re, probe_im, measured,
    right_fwd, left_fwd, left_inv, right_inv,
    numer, grads,
    patch, power, far,
):
    slots, extent = measured.shape[0], measured.shape[1]
    modes = probe_re.shape[0]
    capacity = slots // counts.shape[0]
    numer[...] = jnp.zeros_like(numer)
    grads[...] = jnp.zeros_like(grads)
    lane = lax.broadcasted_iota(jnp.int32, (extent, LANES), 1)
    summed = probe_re[0] * probe_re[0] + probe_im[0] * probe_im[0]
    for m in range(1, modes):
        summed = summed + probe_re[m] * probe_re[m] + probe_im[m] * probe_im[m]
    power[...] = summed

    def visit(slot, carry):
        alive = slot % capacity < counts[slot // capacity]

        @pl.when(alive)
        def _():
            row = offsets[slot, 0]
            col = offsets[slot, 1]
            block = col // LANES
            inner = col % LANES
            rows = pl.ds(row, extent)
            back = lax.rem(LANES - inner, LANES)

            def cut(wide):
                first = pltpu.roll(wide[block, rows, :], back, 1)
                second = pltpu.roll(wide[block + 1, rows, :], back, 1)
                return jnp.where(lane < LANES - inner, first, second)

            patch[0] = cut(wide_re)
            patch[1] = cut(wide_im)
            total = jnp.zeros((extent, extent), F32)
            for m in range(0, modes, 2):
                mids = []
                for n in (m, m + 1):
                    a, b = patch[0], patch[1]
                    p, q = probe_re[n], probe_im[n]
                    mids.append(right_product(p * a - q * b, p * b + q * a, right_fwd[...]))
                wide_real = jnp.concatenate([y[:, :extent] for y in mids], axis=1)
                wide_imag = jnp.concatenate([y[:, extent:] for y in mids], axis=1)
                z = left_product(left_fwd[...], wide_real, wide_imag)
                far[m // 2] = z
                s = z[:extent] * z[:extent] + z[extent:] * z[extent:]
                total = total + s[:, :extent] + s[:, extent:]
            factor = jnp.sqrt(measured[slot]) / jnp.sqrt(jnp.maximum(total, 1.0)) - 1.0
            both = jnp.concatenate([factor, factor], axis=1)
            up_re = jnp.zeros((extent, extent), F32)
            up_im = jnp.zeros((extent, extent), F32)
            for m in range(0, modes, 2):
                z = far[m // 2]
                g = left_product(left_inv[...], z[:extent] * both, z[extent:] * both)
                for n in (m, m + 1):
                    cut_n = slice((n - m) * extent, (n - m + 1) * extent)
                    chi = right_product(g[:extent, cut_n], g[extent:, cut_n], right_inv[...])
                    c, d = chi[:, :extent], chi[:, extent:]
                    a, b = patch[0], patch[1]
                    p, q = probe_re[n], probe_im[n]
                    up_re = up_re + p * c + q * d
                    up_im = up_im + p * d - q * c
                    grads[n] += a * c + b * d
                    grads[modes + n] += a * d - b * c
            a, b = patch[0], patch[1]
            grads[2 * modes] += a * a + b * b

            def place(plane, piece):
                moved = pltpu.roll(piece, inner, 1)
                numer[plane, block, rows, :] += jnp.where(lane >= inner, moved, 0.0)
                numer[plane, block + 1, rows, :] += jnp.where(lane < inner, moved, 0.0)

            place(0, up_re)
            place(1, up_im)
            place(2, power[...])

        return carry

    lax.fori_loop(0, slots, visit, 0)


def local_work(
    offsets, counts, wide_re, wide_im, probe_re, probe_im, measured, grad_planes
):
    modes, extent = probe_re.shape[0], probe_re.shape[1]
    tables = dft_tables(extent)
    vmem = pl.BlockSpec(memory_space=pltpu.VMEM)
    smem = pl.BlockSpec(memory_space=pltpu.SMEM)
    return pl.pallas_call(
        main_kernel,
        out_shape=(
            jax.ShapeDtypeStruct((3,) + wide_re.shape, F32),
            jax.ShapeDtypeStruct((grad_planes, extent, extent), F32),
        ),
        in_specs=[smem, smem] + [vmem] * 9,
        out_specs=(vmem,) * 2,
        scratch_shapes=[
            pltpu.VMEM((2, extent, extent), F32),
            pltpu.VMEM((extent, extent), F32),
            pltpu.VMEM((modes // 2, 2 * extent, 2 * extent), F32),
        ],
        compiler_params=pltpu.CompilerParams(vmem_limit_bytes=48 * 1024 * 1024),
        name="local_work",
    )(offsets, counts, wide_re, wide_im, probe_re, probe_im, measured, *tables)


def greet(partners):
    barrier = pltpu.get_barrier_semaphore()
    for partner in partners:
        pl.semaphore_signal(barrier, inc=1, device_id=partner, device_id_type=pl.DeviceIdType.MESH)
    pl.semaphore_wait(barrier, len(partners))


def remote(src, dst, send, recv, partner):
    return pltpu.make_async_remote_copy(
        src_ref=src, dst_ref=dst, send_sem=send, recv_sem=recv,
        device_id=partner, device_id_type=pl.DeviceIdType.MESH,
    )


def first_exchange_kernel(
    n_ty, n_tx, obj_re, obj_im, patterns, wide_re, wide_im, measured,
    rim_send, rim_recv, scan_send, scan_recv, own_sem,
):
    ty, tx = lax.axis_index("ty"), lax.axis_index("tx")
    height, width = obj_re.shape
    extent = patterns.shape[1]
    blocks = width // LANES
    capacity = patterns.shape[0] // n_tx
    up, down = lax.rem(ty + n_ty - 1, n_ty), lax.rem(ty + 1, n_ty)
    left, right = lax.rem(tx + n_tx - 1, n_tx), lax.rem(tx + 1, n_tx)
    peers = [lax.rem(tx + d, n_tx) for d in range(1, n_tx)]
    greet(
        [(ty, p) for p in peers]
        + [(up, tx), (down, tx), (up, left), (down, right)]
    )
    rims = []
    for plane, (obj, wide) in enumerate(((obj_re, wide_re), (obj_im, wide_im))):
        base = plane * (blocks + 2)
        top = pl.ds(0, extent)
        below = pl.ds(height, extent)
        rims.append((
            obj.at[:, pl.ds(0, LANES)], wide.at[blocks, pl.ds(0, height), :], base,
            (ty, left), tx > 0, tx < n_tx - 1,
        ))
        for b in range(blocks):
            rims.append((
                obj.at[top, pl.ds(b * LANES, LANES)], wide.at[b, below, :], base + 1 + b,
                (up, tx), ty > 0, ty < n_ty - 1,
            ))
        rims.append((
            obj.at[top, pl.ds(0, LANES)], wide.at[blocks, below, :], base + 1 + blocks,
            (up, left), jnp.logical_and(tx > 0, ty > 0),
            jnp.logical_and(tx < n_tx - 1, ty < n_ty - 1),
        ))

    for src, dst, sem, partner, sends, takes in rims:
        @pl.when(sends)
        def _():
            remote(src, dst, rim_send.at[sem], rim_recv.at[sem], partner).start()

    def scan_copy(d):
        peer = peers[d - 1]
        return remote(
            patterns.at[pl.ds(peer * capacity, capacity)],
            measured.at[pl.ds(tx * capacity, capacity)],
            scan_send.at[d - 1], scan_recv.at[d - 1], (ty, peer),
        )

    for d in range(1, n_tx):
        scan_copy(d).start()
    own = pl.ds(tx * capacity, capacity)
    own_copy = pltpu.make_async_copy(patterns.at[own], measured.at[own], own_sem)
    own_copy.start()
    for obj, wide in ((obj_re, wide_re), (obj_im, wide_im)):
        for b in range(blocks):
            wide[b, :height, :] = obj[:, b * LANES : (b + 1) * LANES]
        for dst, absent in (
            (wide.at[blocks, pl.ds(0, height), :], tx == n_tx - 1),
            (wide.at[pl.ds(0, blocks), pl.ds(height, extent), :], ty == n_ty - 1),
            (
                wide.at[blocks, pl.ds(height, extent), :],
                jnp.logical_or(tx == n_tx - 1, ty == n_ty - 1),
            ),
        ):
            @pl.when(absent)
            def _():
                dst[...] = jnp.zeros(dst.shape, F32)

    own_copy.wait()
    for src, dst, sem, partner, sends, takes in rims:
        @pl.when(sends)
        def _():
            remote(src, dst, rim_send.at[sem], rim_recv.at[sem], partner).wait_send()

        @pl.when(takes)
        def _():
            remote(src, dst, rim_send.at[sem], rim_recv.at[sem], partner).wait_recv()

    for d in range(1, n_tx):
        source = lax.rem(tx + n_tx - d, n_tx)
        scan_copy(d).wait_send()
        remote(
            patterns.at[pl.ds(source * capacity, capacity)],
            measured.at[pl.ds(source * capacity, capacity)],
            scan_send.at[d - 1], scan_recv.at[d - 1], (ty, source),
        ).wait_recv()


def first_exchange(n_ty, n_tx, obj_re, obj_im, patterns):
    height, width = obj_re.shape
    extent = patterns.shape[1]
    blocks = width // LANES
    vmem = pl.BlockSpec(memory_space=pltpu.VMEM)
    wide = jax.ShapeDtypeStruct((blocks + 1, height + extent, LANES), F32)
    count = 2 * (blocks + 2)
    return pl.pallas_call(
        lambda *refs: first_exchange_kernel(n_ty, n_tx, *refs),
        out_shape=(wide, wide, jax.ShapeDtypeStruct(patterns.shape, F32)),
        in_specs=[vmem] * 3,
        out_specs=(vmem,) * 3,
        scratch_shapes=[
            pltpu.SemaphoreType.DMA((count,)),
            pltpu.SemaphoreType.DMA((count,)),
            pltpu.SemaphoreType.DMA((n_tx - 1,)),
            pltpu.SemaphoreType.DMA((n_tx - 1,)),
            pltpu.SemaphoreType.DMA,
        ],
        compiler_params=pltpu.CompilerParams(
            collective_id=0, has_side_effects=True, vmem_limit_bytes=48 * 1024 * 1024
        ),
        name="comm_first",
    )(obj_re, obj_im, patterns)


def stages_of(n_ty, n_tx):
    wanted = [("ty", 1, 2), ("ty", 2, n_ty // 2), ("tx", 1, 2), ("tx", 2, n_tx // 2)]
    return [stage for stage in wanted if stage[2] > 1]


def last_exchange_kernel(
    n_ty, n_tx, modes, numer, grads, obj_re, obj_im, probe_re, probe_im,
    new_re, new_im, new_probe_re, new_probe_im,
    beside, below, corner, result, halo_send, halo_recv, *scratch,
):
    stages = stages_of(n_ty, n_tx)
    depth = len(stages)
    received = scratch[:depth]
    partial = scratch[depth : 2 * depth - 1]
    send_sems, recv_sems, back_send, back_recv = scratch[2 * depth - 1 :]
    ty, tx = lax.axis_index("ty"), lax.axis_index("tx")
    height, width = obj_re.shape
    extent = probe_re.shape[1]
    blocks = width // LANES
    up, down = lax.rem(ty + n_ty - 1, n_ty), lax.rem(ty + 1, n_ty)
    left, right = lax.rem(tx + n_tx - 1, n_tx), lax.rem(tx + 1, n_tx)

    def member(stage):
        axis, stride, size = stage
        return lax.rem((ty if axis == "ty" else tx) // stride, size)

    def peer(stage, shift):
        axis, stride, size = stage
        q = member(stage)
        other = lax.rem(q + shift + size, size)
        if axis == "ty":
            return other, (ty + (other - q) * stride, tx)
        return other, (ty, tx + (other - q) * stride)

    partners = [(ty, left), (ty, right), (up, tx), (down, tx), (up, left), (down, right)]
    for stage in stages:
        for d in range(1, stage[2]):
            partners.append(peer(stage, d)[1])
    greet(partners)

    halos = (
        (numer.at[:, blocks, pl.ds(0, height), :], beside, 0, (ty, right),
         tx < n_tx - 1, tx > 0),
        (numer.at[:, pl.ds(0, blocks), pl.ds(height, extent), :], below, 1, (down, tx),
         ty < n_ty - 1, ty > 0),
        (numer.at[:, blocks, pl.ds(height, extent), :], corner, 2, (down, right),
         jnp.logical_and(tx < n_tx - 1, ty < n_ty - 1), jnp.logical_and(tx > 0, ty > 0)),
    )

    def halo_copy(halo):
        src, dst, sem, partner = halo[:4]
        return remote(src, dst, halo_send.at[sem], halo_recv.at[sem], partner)

    def start_halos(chosen):
        for halo in chosen:
            @pl.when(halo[4])
            def _():
                halo_copy(halo).start()

    power = probe_re[0] * probe_re[0] + probe_im[0] * probe_im[0]
    for m in range(1, modes):
        power = power + probe_re[m] * probe_re[m] + probe_im[m] * probe_im[m]
    floor = 0.1 * jnp.max(power)

    def update_object(b, r):
        cols = slice(b * LANES, (b + 1) * LANES)
        band = slice(r, r + extent)
        sums = []
        for plane in range(3):
            value = numer[plane, b, band, :]
            if r == 0:
                value = value + below[plane, b]
            if b == 0:
                value = value + beside[plane, band, :]
            if r == 0 and b == 0:
                value = value + corner[plane]
            sums.append(value)
        weight = sums[2] + floor
        new_re[band, cols] = obj_re[band, cols] + sums[0] / weight
        new_im[band, cols] = obj_im[band, cols] + sums[1] / weight

    rows = grads.shape[0]
    lengths = [rows]
    for stage in stages:
        lengths.append(lengths[-1] // stage[2])
    firsts = [0]
    while len(firsts) <= depth:
        firsts.append(firsts[-1] + (stages[len(firsts) - 1][2] - 1))
    source = grads
    base = jnp.int32(0)
    for s, stage in enumerate(stages):
        length = lengths[s + 1]
        copies = []
        for d in range(1, stage[2]):
            other, device = peer(stage, d)
            sem = firsts[s] + d - 1
            copies.append(remote(
                source.at[pl.ds(pl.multiple_of(other * length, 8), length), :],
                received[s].at[d - 1],
                send_sems.at[sem], recv_sems.at[sem], device,
            ))
        for copy in copies:
            copy.start()
        if s == 0:
            start_halos(halos[:1])
        if s == 1:
            for b in range(1, blocks):
                for r in range(extent, height, extent):
                    update_object(b, r)
        for copy in copies:
            copy.wait()
        if s == 1:
            start_halos(halos[1:])
        q = member(stage)
        total = source[pl.ds(pl.multiple_of(q * length, 8), length), :]
        for d in range(1, stage[2]):
            total = total + received[s][d - 1]
        base = base + q * length
        if s < depth - 1:
            source = partial[s]
            source[...] = total
        else:
            result[pl.ds(pl.multiple_of(base, 8), length), :] = total
    pending = []
    for s in range(depth - 1, -1, -1):
        stage, length = stages[s], lengths[s + 1]
        held = result.at[pl.ds(pl.multiple_of(base, 8), length), :]
        copies = []
        for d in range(1, stage[2]):
            other, device = peer(stage, d)
            sem = firsts[s] + d - 1
            copy = remote(held, held, back_send.at[sem], back_recv.at[sem], device)
            copy.start()
            copies.append(copy)
        q = member(stage)
        for d in range(1, stage[2]):
            other, device = peer(stage, -d)
            sem = firsts[s] + d - 1
            place = result.at[pl.ds(pl.multiple_of(base + (other - q) * length, 8), length), :]
            remote(place, place, back_send.at[sem], back_recv.at[sem], device).wait_recv()
        pending += copies
        base = base - q * length
    for copy in pending:
        copy.wait_send()

    norm = result[pl.ds(2 * modes * extent, extent), :] + 1.0
    for m in range(modes):
        real = result[pl.ds(m * extent, extent), :]
        imag = result[pl.ds((modes + m) * extent, extent), :]
        new_probe_re[m] = probe_re[m] + real / norm
        new_probe_im[m] = probe_im[m] + imag / norm

    for halo in halos:
        @pl.when(halo[4])
        def _():
            halo_copy(halo).wait_send()

        @pl.when(halo[5])
        def _():
            halo_copy(halo).wait_recv()

    for halo in halos:
        @pl.when(jnp.logical_not(halo[5]))
        def _():
            halo[1][...] = jnp.zeros(halo[1].shape, F32)

    for b in range(blocks):
        for r in range(0, height, extent):
            if b == 0 or r == 0:
                update_object(b, r)


def last_exchange(n_ty, n_tx, numer, grads, obj_re, obj_im, probe_re, probe_im):
    modes, extent = probe_re.shape[0], probe_re.shape[1]
    height, width = obj_re.shape
    blocks = width // LANES
    stages = stages_of(n_ty, n_tx)
    rows = grads.shape[0]
    vmem = pl.BlockSpec(memory_space=pltpu.VMEM)
    received, partial = [], []
    length = rows
    for stage in stages:
        length = length // stage[2]
        received.append(pltpu.VMEM((stage[2] - 1, length, LANES), F32))
        partial.append(pltpu.VMEM((length, LANES), F32))
    count = sum(stage[2] - 1 for stage in stages)
    tile = jax.ShapeDtypeStruct(obj_re.shape, F32)
    wave = jax.ShapeDtypeStruct(probe_re.shape, F32)
    return pl.pallas_call(
        lambda *refs: last_exchange_kernel(n_ty, n_tx, modes, *refs),
        out_shape=(tile, tile, wave, wave),
        in_specs=[vmem] * 6,
        out_specs=(vmem,) * 4,
        scratch_shapes=[
            pltpu.VMEM((3, height, LANES), F32),
            pltpu.VMEM((3, blocks, extent, LANES), F32),
            pltpu.VMEM((3, extent, LANES), F32),
            pltpu.VMEM((rows, LANES), F32),
            pltpu.SemaphoreType.DMA((3,)),
            pltpu.SemaphoreType.DMA((3,)),
            *received,
            *partial[:-1],
            *[pltpu.SemaphoreType.DMA((count,))] * 4,
        ],
        compiler_params=pltpu.CompilerParams(
            collective_id=1, has_side_effects=True, vmem_limit_bytes=48 * 1024 * 1024
        ),
        name="comm_last",
    )(numer, grads, obj_re, obj_im, probe_re, probe_im)


def body(object_re, object_im, probe_re, probe_im, patterns, offsets, counts):
    n_ty, n_tx = lax.axis_size("ty"), lax.axis_size("tx")
    modes, extent = probe_re.shape[0], probe_re.shape[1]
    wide_re, wide_im, measured = first_exchange(n_ty, n_tx, object_re, object_im, patterns[0, 0])
    rows = (2 * modes + 1) * extent
    unit = 8 * n_ty * n_tx
    unit = unit * extent // math.gcd(unit, extent)
    grad_planes = -(-rows // unit) * unit // extent
    numer, grads = local_work(
        offsets[0, 0], counts[0, 0], wide_re, wide_im, probe_re, probe_im, measured, grad_planes
    )
    return last_exchange(
        n_ty, n_tx, numer, grads.reshape(grad_planes * extent, extent),
        object_re, object_im, probe_re, probe_im,
    )


def solution(mesh):
    return jax.shard_map(
        body,
        mesh=mesh,
        in_specs=(
            P("ty", "tx"),
            P("ty", "tx"),
            P(),
            P(),
            P("ty", "tx", None, None, None),
            P("ty", "tx", None, None),
            P("ty", "tx", None),
        ),
        out_specs=(P("ty", "tx"), P("ty", "tx"), P(), P()),
        check_vma=False,
    )
```

profile of v0, /device:TPU:0, one launch (start us, length us, event | category | flops | bytes accessed | tf_op | source)
XLA Modules:
  0.0 148.2 jit_solution(7813258693586376736)
XLA Ops:
  0.6 0.0 copy-start.12
  0.6 0.8 copy.15.offsets
  1.4 0.0 copy-start
  1.4 1.2 copy-done
  2.6 0.0 copy-start.2
  2.6 1.2 copy-done.2
  3.9 0.0 copy-start.7
  3.9 1.2 copy-done.7
  5.1 0.0 copy-start.3
  5.1 0.0 copy-start.4
  5.1 0.0 copy-start.8
  5.1 0.0 copy-start.10
  5.1 0.0 copy-start.11
  5.1 31.7 %comm_first.1 = (f32[5,640,128]{2,1,0:T(8,128)S(1)}, f32[5,640,128]{2,1,0:T(8,128)}, f32[16,128,128]{2,1,0:T(8,128)S(1)}) custom-call(f32[512,512]{1,0:T(8,128)S(1)} %copy-done, f32[512,512]{1,0:T(8,128)S(1)} %copy-done.2, f32[16,128,128]{2,1,0:T(8,128)S(1)} %bitcast.5), custom_call_target="tpu_custom_call" | custom-call | tf_op jit(solution)/shard_map/comm_first/pallas_call | solution.py:276
  36.8 0.0 copy-start.5
  36.8 1.2 copy-done.5
  38.0 0.0 copy-done.12
  38.0 0.0 copy-done.3
  38.0 0.0 copy-done.4
  38.0 0.0 copy-done.8
  38.0 0.0 copy-done.9
  38.0 0.0 copy-done.10
  38.0 0.0 copy-done.11
  38.1 0.0 copy-start.1
  38.1 37.6 %local_work.1 = (f32[3,5,640,128]{3,2,1,0:T(8,128)}, f32[18,128,128]{2,1,0:T(8,128)S(1)}) custom-call(s32[16,2]{1,0:T(8,128)S(1)} %copy.15.offsets, s32[8]{0:T(128)S(1)} %bitcast.6, f32[5,640,128]{2,1,0:T(8,128)} %copy-done.5, f32[5,640,128]{2,1,0:T(8,128)} %get-tuple-element.10.wide_im, f32[8,128,128]{2,1,0:T(8,128)S(1)} %copy-done.3, ...), custom_call_target="tpu_custom_call" | custom-call | tf_op jit(solution)/shard_map/local_work/pallas_call | solution.py:148
  75.6 1.0 copy-done.6
  76.7 0.0 copy-done.1
  76.7 68.0 %comm_last.1 = (f32[512,512]{1,0:T(8,128)S(1)}, f32[512,512]{1,0:T(8,128)S(1)}, f32[8,128,128]{2,1,0:T(8,128)S(1)}, f32[8,128,128]{2,1,0:T(8,128)S(1)}) custom-call(f32[3,5,640,128]{3,2,1,0:T(8,128)} %get-tuple-element.12.refs_0_, f32[2304,128]{1,0:T(8,128)} %bitcast.4, f32[512,512]{1,0:T(8,128)S(1)} %copy-done.1, f32[512,512]{1,0:T(8,128)} %refs_3_.1, ...), custom_call_target="tpu_custom_call" | custom-call | tf_op jit(solution)/shard_map/comm_last/pallas_call | solution.py:483
  144.7 1.0 copy.20
  145.6 1.0 copy.21
  146.6 0.8 copy.22
  147.4 0.8 copy.23
  (2 shorter events, 0.0 us)
Async XLA Ops:
  0.6 37.4 %copy-start.12 = (s32[1,1,8]{2,1,0:T(1,128)S(1)}, s32[1,1,8]{2,1,0:T(1,128)}, u32[]{:S(2)}) copy-start(s32[1,1,8]{2,1,0:T(1,128)} %param.17) | copy-start | bytes 100
  1.4 1.2 copy-start
  2.6 1.2 copy-start.2
  3.9 1.2 copy-start.7
  5.1 32.9 %copy-start.3 = (f32[8,128,128]{2,1,0:T(8,128)S(1)}, f32[8,128,128]{2,1,0:T(8,128)}, u32[]{:S(2)}) copy-start(f32[8,128,128]{2,1,0:T(8,128)} %refs_4_.1) | copy-start | bytes 1572868
  5.1 32.9 %copy-start.4 = (f32[8,128,128]{2,1,0:T(8,128)S(1)}, f32[8,128,128]{2,1,0:T(8,128)}, u32[]{:S(2)}) copy-start(f32[8,128,128]{2,1,0:T(8,128)} %refs_5_.1) | copy-start | bytes 1572868
  5.1 32.9 %copy-start.8 = (bf16[768,256]{1,0:T(8,128)(2,1)S(1)}, bf16[768,256]{1,0:T(8,128)(2,1)}, u32[]{:S(2)}) copy-start(bf16[768,256]{1,0:T(8,128)(2,1)} %constant.11.clone.right_inv) | copy-start | bytes 1179652
  5.1 32.9 %copy-start.9 = (bf16[256,768]{1,0:T(8,128)(2,1)S(1)}, bf16[256,768]{1,0:T(8,128)(2,1)}, u32[]{:S(2)}) copy-start(bf16[256,768]{1,0:T(8,128)(2,1)} %constant.10.clone.left_inv) | copy-start | bytes 1179652
  5.1 32.9 %copy-start.10 = (bf16[256,768]{1,0:T(8,128)(2,1)S(1)}, bf16[256,768]{1,0:T(8,128)(2,1)}, u32[]{:S(2)}) copy-start(bf16[256,768]{1,0:T(8,128)(2,1)} %constant.9.clone.left_fwd) | copy-start | bytes 1179652
  5.1 32.9 %copy-start.11 = (bf16[768,256]{1,0:T(8,128)(2,1)S(1)}, bf16[768,256]{1,0:T(8,128)(2,1)}, u32[]{:S(2)}) copy-start(bf16[768,256]{1,0:T(8,128)(2,1)} %constant.8.clone.right_fwd) | copy-start | bytes 1179652
  36.8 1.2 copy-start.5
  38.1 38.6 %copy-start.1 = (f32[512,512]{1,0:T(8,128)S(1)}, f32[512,512]{1,0:T(8,128)}, u32[]{:S(2)}) copy-start(f32[512,512]{1,0:T(8,128)} %refs_2_.1) | copy-start | bytes 3145732
  75.6 1.0 copy-start.6
where the time goes:
time: 150 us; the launch traced here: 148 us
  Pallas kernels  137 us (91%)
  local copies, waits for them, and re-layouts  10.2 us (7%)
    pallas_call x1, Pallas kernels, last_exchange(): pl.pallas_call(lambda *refs: last_exchange_kernel(n_ty, n_tx, modes, *ref...  68 us
    pallas_call x1, Pallas kernels, local_work(): pl.pallas_call(main_kernel, out_shape=(jax.ShapeDtypeStruct((3,) + wide_r...  37.6 us
    pallas_call x1, Pallas kernels, first_exchange(): pl.pallas_call(lambda *refs: first_exchange_kernel(n_ty, n_tx, *refs), ou...  31.7 us
    unnamed x30, local copies, waits for them, and re-layouts  9.44 us

commit v1 on v0

--- a/solution.py
+++ b/solution.py
@@ -213,11 +213,6 @@
             jnp.logical_and(tx < n_tx - 1, ty < n_ty - 1),
         ))
 
-    for src, dst, sem, partner, sends, takes in rims:
-        @pl.when(sends)
-        def _():
-            remote(src, dst, rim_send.at[sem], rim_recv.at[sem], partner).start()
-
     def scan_copy(d):
         peer = peers[d - 1]
         return remote(
@@ -228,6 +223,12 @@
 
     for d in range(1, n_tx):
         scan_copy(d).start()
+
+    for src, dst, sem, partner, sends, takes in rims:
+        @pl.when(sends)
+        def _():
+            remote(src, dst, rim_send.at[sem], rim_recv.at[sem], partner).start()
+
     own = pl.ds(tx * capacity, capacity)
     own_copy = pltpu.make_async_copy(patterns.at[own], measured.at[own], own_sem)
     own_copy.start()

time: 150 us -> 142 us (0.947); the launches traced: 148 us -> 142 us
  Pallas kernels: 137 us -> 131 us
    pallas_call x1, Pallas kernels: 37.6 us -> 28.7 us  [local_work(): pl.pallas_call(main_kernel, out_shape=(jax.ShapeDtypeStruct((3,) + wide_r...]
    pallas_call x1, Pallas kernels: 68 us -> 69.9 us  [last_exchange(): pl.pallas_call(lambda *refs: last_exchange_kernel(n_ty, n_tx, modes, *ref...]
where the time goes in v1:
time: 142 us
  Pallas kernels  131 us (92%)
  local copies, waits for them, and re-layouts  10.2 us (7%)
    pallas_call x1, Pallas kernels, last_exchange(): pl.pallas_call(lambda *refs: last_exchange_kernel(n_ty, n_tx, modes, *ref...  69.9 us
    pallas_call x1, Pallas kernels, first_exchange(): pl.pallas_call(lambda *refs: first_exchange_kernel(n_ty, n_tx, *refs), ou...  32.5 us
    pallas_call x1, Pallas kernels, local_work(): pl.pallas_call(main_kernel, out_shape=(jax.ShapeDtypeStruct((3,) + wide_r...  28.7 us
    unnamed x30, local copies, waits for them, and re-layouts  9.44 us

profile of v1, /device:TPU:0, one launch (start us, length us, event | category | flops | bytes accessed | tf_op | source)
XLA Modules:
  0.0 141.9 jit_solution(11175476280651771419)
XLA Ops:
  0.6 0.0 copy-start.12
  0.6 0.8 copy.15.offsets
  1.4 0.0 copy-start
  1.4 1.2 copy-done
  2.6 0.0 copy-start.2
  2.6 1.2 copy-done.2
  3.9 0.0 copy-start.7
  3.9 1.2 copy-done.7
  5.1 0.0 copy-start.3
  5.1 0.0 copy-start.8
  5.1 0.0 copy-start.9
  5.1 0.0 copy-start.10
  5.1 0.0 copy-start.11
  5.1 32.5 %comm_first.1 = (f32[5,640,128]{2,1,0:T(8,128)S(1)}, f32[5,640,128]{2,1,0:T(8,128)}, f32[16,128,128]{2,1,0:T(8,128)S(1)}) custom-call(f32[512,512]{1,0:T(8,128)S(1)} %copy-done, f32[512,512]{1,0:T(8,128)S(1)} %copy-done.2, f32[16,128,128]{2,1,0:T(8,128)S(1)} %bitcast.5), custom_call_target="tpu_custom_call" | custom-call | tf_op jit(solution)/shard_map/comm_first/pallas_call | solution.py:277
  37.6 0.0 copy-start.5
  37.6 1.2 copy-done.5
  38.8 0.0 copy-done.12
  38.8 0.0 copy-done.3
  38.8 0.0 copy-done.4
  38.8 0.0 copy-done.8
  38.8 0.0 copy-done.9
  38.8 0.0 copy-done.10
  38.8 0.0 copy-done.11
  38.8 0.0 copy-start.1
  38.8 28.7 %local_work.1 = (f32[3,5,640,128]{3,2,1,0:T(8,128)}, f32[18,128,128]{2,1,0:T(8,128)S(1)}) custom-call(s32[16,2]{1,0:T(8,128)S(1)} %copy.15.offsets, s32[8]{0:T(128)S(1)} %bitcast.6, f32[5,640,128]{2,1,0:T(8,128)} %copy-done.5, f32[5,640,128]{2,1,0:T(8,128)} %get-tuple-element.10.wide_im, f32[8,128,128]{2,1,0:T(8,128)S(1)} %copy-done.3, ...), custom_call_target="tpu_custom_call" | custom-call | tf_op jit(solution)/shard_map/local_work/pallas_call | solution.py:148
  67.5 1.0 copy-done.6
  68.5 0.0 copy-done.1
  68.6 69.9 %comm_last.1 = (f32[512,512]{1,0:T(8,128)S(1)}, f32[512,512]{1,0:T(8,128)S(1)}, f32[8,128,128]{2,1,0:T(8,128)S(1)}, f32[8,128,128]{2,1,0:T(8,128)S(1)}) custom-call(f32[3,5,640,128]{3,2,1,0:T(8,128)} %get-tuple-element.12.refs_0_, f32[2304,128]{1,0:T(8,128)} %bitcast.4, f32[512,512]{1,0:T(8,128)S(1)} %copy-done.1, f32[512,512]{1,0:T(8,128)} %refs_3_.1, ...), custom_call_target="tpu_custom_call" | custom-call | tf_op jit(solution)/shard_map/comm_last/pallas_call | solution.py:484
  138.4 1.0 copy.20
  139.4 1.0 copy.21
  140.4 0.8 copy.22
  141.2 0.8 copy.23
  (2 shorter events, 0.0 us)
Async XLA Ops:
  0.6 38.2 %copy-start.12 = (s32[1,1,8]{2,1,0:T(1,128)S(1)}, s32[1,1,8]{2,1,0:T(1,128)}, u32[]{:S(2)}) copy-start(s32[1,1,8]{2,1,0:T(1,128)} %param.17) | copy-start | bytes 100
  1.4 1.2 copy-start
  2.6 1.2 copy-start.2
  3.9 1.2 copy-start.7
  5.1 33.7 %copy-start.3 = (f32[8,128,128]{2,1,0:T(8,128)S(1)}, f32[8,128,128]{2,1,0:T(8,128)}, u32[]{:S(2)}) copy-start(f32[8,128,128]{2,1,0:T(8,128)} %refs_4_.1) | copy-start | bytes 1572868
  5.1 33.7 %copy-start.4 = (f32[8,128,128]{2,1,0:T(8,128)S(1)}, f32[8,128,128]{2,1,0:T(8,128)}, u32[]{:S(2)}) copy-start(f32[8,128,128]{2,1,0:T(8,128)} %refs_5_.1) | copy-start | bytes 1572868
  5.1 33.7 %copy-start.8 = (bf16[768,256]{1,0:T(8,128)(2,1)S(1)}, bf16[768,256]{1,0:T(8,128)(2,1)}, u32[]{:S(2)}) copy-start(bf16[768,256]{1,0:T(8,128)(2,1)} %constant.11.clone.right_inv) | copy-start | bytes 1179652
  5.1 33.7 %copy-start.9 = (bf16[256,768]{1,0:T(8,128)(2,1)S(1)}, bf16[256,768]{1,0:T(8,128)(2,1)}, u32[]{:S(2)}) copy-start(bf16[256,768]{1,0:T(8,128)(2,1)} %constant.10.clone.left_inv) | copy-start | bytes 1179652
  5.1 33.7 %copy-start.10 = (bf16[256,768]{1,0:T(8,128)(2,1)S(1)}, bf16[256,768]{1,0:T(8,128)(2,1)}, u32[]{:S(2)}) copy-start(bf16[256,768]{1,0:T(8,128)(2,1)} %constant.9.clone.left_fwd) | copy-start | bytes 1179652
  5.1 33.7 %copy-start.11 = (bf16[768,256]{1,0:T(8,128)(2,1)S(1)}, bf16[768,256]{1,0:T(8,128)(2,1)}, u32[]{:S(2)}) copy-start(bf16[768,256]{1,0:T(8,128)(2,1)} %constant.8.clone.right_fwd) | copy-start | bytes 1179652
  37.6 1.2 copy-start.5
  38.8 29.7 %copy-start.1 = (f32[512,512]{1,0:T(8,128)S(1)}, f32[512,512]{1,0:T(8,128)}, u32[]{:S(2)}) copy-start(f32[512,512]{1,0:T(8,128)} %refs_2_.1) | copy-start | bytes 3145732
  67.5 1.0 copy-start.6
